TPU v7x, 32 devices: a whole 2x2x4 slice. The times are simulated.
32 devices in a mesh: scene: 8 (over z, y), seq: 4 (over x, core).
Axes of the slice: x: 2, y: 2, z: 4, core: 2. Of those that a mesh axis runs over, the one named last changes fastest.
Arguments:
- scene_x: bfloat16 [8, 65536, 256], P('scene', 'seq'), may hold values from -6 to 6
- cotangent: bfloat16 [8, 65536, 256], P('scene', 'seq'), may hold values from -6 to 6
- gate_gain: float32 [256], replicated, may hold values from 0.3 to 3
- kernel: bfloat16 [256, 256, 256], P(None, 'seq'), may hold values from -6 to 6
- block_mix: bfloat16 [256, 256], replicated, may hold values from -0.375 to 0.375
- across_mix: bfloat16 [256, 256], replicated, may hold values from -0.375 to 0.375
- across_unmix: bfloat16 [256, 256], replicated, may hold values from -0.375 to 0.375
- block_unmix: bfloat16 [256, 256], replicated, may hold values from -0.375 to 0.375
Outputs:
- mixed: bfloat16 [8, 65536, 256], P('scene', 'seq')
- grad_x: bfloat16 [8, 65536, 256], P('scene', 'seq')
- grad_kernel: float32 [256, 256, 256], P('scene', 'seq')
- grad_gain: float32 [256], replicated
All inputs are finite; a program needn't handle non-finite values.
Results may differ from a plain program's by a relative error of at most 0.007.
Values may be sent and summed in bfloat16 or wider, within the bound.
A program may use at most 192 MiB of HBM per device.

v0:
```python
import jax
import jax.numpy as jnp
from jax import lax
from jax.sharding import PartitionSpec as P


def on_device(
    scene_x, cotangent, gate_gain, kernel, block_mix, across_mix, across_unmix, block_unmix
):
    f32 = jnp.float32
    bf16 = jnp.bfloat16
    scenes_here, row_count, channels = scene_x.shape
    block_len = block_mix.shape[0]
    local_a = row_count // block_len
    kernel_f = kernel.astype(f32)
    inputs = scene_x.reshape(scenes_here, local_a, block_len, channels)
    first_mix = jnp.einsum("jb,sabc->sajc", block_mix, inputs, preferred_element_type=f32).astype(
        bf16
    )
    spread_mix = lax.all_to_all(first_mix, "seq", split_axis=2, concat_axis=1, tiled=True)
    second_mix = jnp.einsum(
        "ia,sajc->sijc", across_mix, spread_mix, preferred_element_type=f32
    ).astype(bf16)
    weighted = (second_mix.astype(f32) * kernel_f).astype(bf16)
    unmixed = jnp.einsum(
        "pi,sijc->spjc", across_unmix, weighted, preferred_element_type=f32
    ).astype(bf16)
    returned = lax.all_to_all(unmixed, "seq", split_axis=1, concat_axis=2, tiled=True)
    values = jnp.einsum("qj,spjc->spqc", block_unmix, returned, preferred_element_type=f32)
    gate_pre = inputs.astype(f32) * gate_gain
    gate_sig = jax.nn.sigmoid(gate_pre)
    mixed_out = (
        (values * gate_pre * gate_sig).astype(bf16).reshape(scenes_here, row_count, channels)
    )
    upstream = cotangent.reshape(scenes_here, local_a, block_len, channels).astype(f32)
    grad_values = (upstream * gate_pre * gate_sig).astype(bf16)
    grad_gate = upstream * values * gate_sig * (1.0 + gate_pre * (1.0 - gate_sig))
    grad_unmixed = jnp.einsum(
        "qj,spqc->spjc", block_unmix, grad_values, preferred_element_type=f32
    ).astype(bf16)
    spread_grad = lax.all_to_all(grad_unmixed, "seq", split_axis=2, concat_axis=1, tiled=True)
    grad_weighted = jnp.einsum(
        "pi,spjc->sijc", across_unmix, spread_grad, preferred_element_type=f32
    )
    kernel_term = jnp.sum(grad_weighted * second_mix.astype(f32), axis=0)
    kernel_grad = lax.psum_scatter(kernel_term, "scene", scatter_dimension=0, tiled=True)
    grad_second = (grad_weighted * kernel_f).astype(bf16)
    grad_first = jnp.einsum(
        "ia,sijc->sajc", across_mix, grad_second, preferred_element_type=f32
    ).astype(bf16)
    grad_back = lax.all_to_all(grad_first, "seq", split_axis=1, concat_axis=2, tiled=True)
    grad_input = (
        jnp.einsum("jb,sajc->sabc", block_mix, grad_back, preferred_element_type=f32)
        + grad_gate * gate_gain
    )
    grad_input = grad_input.astype(bf16).reshape(scenes_here, row_count, channels)
    gain_term = jnp.sum(inputs.astype(f32) * grad_gate, axis=(0, 1, 2))
    gain_total = lax.psum(gain_term, ("scene", "seq"))
    total_rows = scenes_here * lax.axis_size("scene") * local_a * lax.axis_size("seq") * block_len
    grad_scale = 1.0 / jnp.sqrt(jnp.float32(total_rows))
    return (mixed_out, grad_input, kernel_grad, gain_total * grad_scale)


def solution(mesh):
    return jax.shard_map(
        on_device,
        mesh=mesh,
        in_specs=(
            P("scene", "seq", None),
            P("scene", "seq", None),
            P(),
            P(None, "seq", None),
            P(),
            P(),
            P(),
            P(),
        ),
        out_specs=(P("scene", "seq", None), P("scene", "seq", None), P("scene", "seq", None), P()),
        check_vma=False,
    )
```

profile of v0, /device:TPU:0, one launch (start us, length us, event | category | flops | bytes accessed | tf_op | source)
XLA Modules:
  0.0 653.9 jit_solution(4546086225329275960)
XLA Ops:
  7.2 0.0 copy-start
  7.2 9.2 %convert_bitcast_fusion.4 = bf16[1,64,256,256]{2,3,1,0:T(8,128)(2,1)} fusion(bf16[64,256,256]{2,1,0:T(8,128)(2,1)} %bitcast.140, bf16[256,256]{1,0:T(8,128)(2,1)} %param.12), kind=kOutput, calls=%fused_computation.39 | convolution fusion | flops 2151677952 | bytes 16908288 | tf_op jit(solution)/shard_map/jb,sabc->sajc/dot_general | solution.py:17
  16.4 12.1 %copy.39 = bf16[1,64,256,256]{3,1,0,2:T(8,128)(2,1)} copy(bf16[1,64,256,256]{2,3,1,0:T(8,128)(2,1)} %convert_bitcast_fusion.4) | data formatting | bytes 16777216 | tf_op jit(solution)/shard_map/convert_element_type | solution.py:17
  28.5 5.6 all-to-all-start
  34.2 11.9 %copy.46 = bf16[64,256,256]{1,2,0:T(8,128)(2,1)} copy(bf16[64,256,256]{2,1,0:T(8,128)(2,1)} %bitcast.141) | data formatting | bytes 16777216 | tf_op jit(solution)/shard_map/reshape
  46.1 9.6 %convert_element_type.152 = f32[1,16384,256]{2,1,0:T(8,128)} convert(bf16[1,16384,256]{2,1,0:T(8,128)(2,1)} %param.9) | non-fusion elementwise | flops 4194304 | bytes 25165824 | tf_op jit(solution)/shard_map/convert_element_type | solution.py:35
  55.7 0.0 copy-start.5
  55.7 17.4 %copy.47 = f32[64,256,256]{1,2,0:T(8,128)} copy(f32[64,256,256]{2,1,0:T(8,128)} %bitcast.144) | data formatting | bytes 33554432 | tf_op jit(solution)/shard_map/convert_element_type | solution.py:35
  73.1 0.0 copy-done
  73.1 0.0 copy-done.5
  73.1 12.8 %convert_bitcast_fusion.2 = bf16[1,64,256,256]{2,3,1,0:T(8,128)(2,1)} fusion(f32[64,256,256]{1,2,0:T(8,128)} %copy.47, bf16[64,256,256]{1,2,0:T(8,128)(2,1)} %copy.46, f32[256]{0:T(256)S(1)} %copy-done.5, bf16[256,256]{1,0:T(8,128)(2,1)S(1)} %copy-done), kind=kOutput, calls=%fused_computation.37 | convolution fusion | flops 2185232384 | bytes 33686528 | tf_op jit(solution)/shard_map/qj,spqc->spjc/dot_general | solution.py:38
  85.9 12.3 %copy.48 = bf16[1,64,256,256]{3,1,0,2:T(8,128)(2,1)} copy(bf16[1,64,256,256]{2,3,1,0:T(8,128)(2,1)} %convert_bitcast_fusion.2) | data formatting | bytes 16777216 | tf_op jit(solution)/shard_map/convert_element_type | solution.py:40
  98.2 29.7 %all-to-all-done = bf16[1,64,256,256]{3,1,0,2:T(8,128)(2,1)} async-done(((bf16[1,64,256,256]{3,1,0,2:T(8,128)(2,1)}), bf16[1,64,256,256]{3,1,0,2:T(8,128)(2,1)}, u32[]{:S(2)}, u32[]{:S(2)}) %all-to-all-start) | async-done | bytes 8388640 | tf_op jit(solution)/shard_map/all_to_all | solution.py:20
  127.9 5.7 all-to-all-start.2
  133.6 0.3 reduce-scatter.2.cloned.1.call-start
  133.9 11.5 %copy.40 = bf16[1,64,256,256]{3,2,1,0:T(8,128)(2,1)} copy(bf16[1,64,256,256]{3,1,0,2:T(8,128)(2,1)} %all-to-all-done) | data formatting | bytes 16777216 | tf_op jit(solution)/shard_map/all_to_all | solution.py:20
  145.4 8.4 %copy.41 = bf16[1,4,64,64,256]{4,3,2,1,0:T(8,128)(2,1)} copy(bf16[1,4,64,64,256]{4,3,1,2,0:T(8,128)(2,1)} %bitcast.148) | data formatting | bytes 16777216 | tf_op jit(solution)/shard_map/all_to_all | solution.py:20
  153.9 72.9 %all-to-all-done.2 = bf16[1,64,256,256]{3,1,0,2:T(8,128)(2,1)} async-done(((bf16[1,64,256,256]{3,1,0,2:T(8,128)(2,1)}), bf16[1,64,256,256]{3,1,0,2:T(8,128)(2,1)}, u32[]{:S(2)}, u32[]{:S(2)}) %all-to-all-start.2) | async-done | bytes 8388640 | tf_op jit(solution)/shard_map/all_to_all | solution.py:41
  226.8 11.5 %copy.49 = bf16[1,64,256,256]{3,2,1,0:T(8,128)(2,1)} copy(bf16[1,64,256,256]{3,1,0,2:T(8,128)(2,1)} %all-to-all-done.2) | data formatting | bytes 16777216 | tf_op jit(solution)/shard_map/all_to_all | solution.py:41
  238.3 0.0 copy-start.3
  238.3 8.3 %copy.50 = bf16[1,4,64,64,256]{4,3,2,1,0:T(8,128)(2,1)} copy(bf16[1,4,64,64,256]{4,3,1,2,0:T(8,128)(2,1)} %bitcast.149) | data formatting | bytes 16777216 | tf_op jit(solution)/shard_map/all_to_all | solution.py:41
  246.6 0.0 copy-done.3
  246.6 0.0 copy-start.2
  246.6 23.9 %fusion.31 = bf16[64,256,256]{2,1,0:T(8,128)(2,1)} fusion(bf16[256,64,256]{2,1,0:T(8,128)(2,1)} %bitcast.147, bf16[256,256]{1,0:T(8,128)(2,1)S(1)} %copy-done.3), kind=kOutput, calls=%fused_computation.41 | convolution fusion | flops 2151677952 | bytes 16908288 | tf_op jit(solution)/shard_map/ia,sajc->sijc/dot_general | solution.py:21
  270.5 0.0 copy-done.2
  270.5 13.5 %fusion.26 = f32[64,256,256]{2,1,0:T(8,128)S(1)} fusion(bf16[256,64,256]{2,1,0:T(8,128)(2,1)} %bitcast.143, bf16[256,256]{1,0:T(8,128)(2,1)S(1)} %copy-done.2), kind=kOutput, calls=%fused_computation.32 | convolution fusion | flops 2147483648 | bytes 25296896 | tf_op jit(solution)/shard_map/pi,spjc->sijc/dot_general | solution.py:42
  284.1 0.0 copy-start.1
  284.1 5.7 copy-done.1
  289.8 10.0 %fusion.15 = f32[256,64,256]{0,2,1:T(8,128)} fusion(f32[64,256,256]{2,1,0:T(8,128)S(1)} %fusion.26, bf16[64,256,256]{2,1,0:T(8,128)(2,1)} %fusion.31), kind=kLoop, calls=%fused_computation.21 | loop fusion | flops 8388608 | bytes 41943040 | tf_op jit(solution)/shard_map/reduce_sum | solution.py:45
  299.8 17.7 %copy.55 = f32[256,64,256]{2,1,0:T(8,128)} copy(f32[256,64,256]{0,2,1:T(8,128)} %fusion.15) | data formatting | bytes 33554432 | tf_op jit(solution)/shard_map/reduce_sum | solution.py:45
  317.5 0.0 reduce-scatter.2.cloned.1.call-update
  317.5 13.0 %copy.43 = bf16[256,64,256]{0,2,1:T(8,128)(2,1)} copy(bf16[256,64,256]{2,1,0:T(8,128)(2,1)} %param.11) | data formatting | bytes 16777216 | tf_op args[3]
  330.5 11.4 %convert_bitcast_fusion.3 = bf16[1,256,64,256]{1,3,2,0:T(8,128)(2,1)} fusion(bf16[64,256,256]{2,1,0:T(8,128)(2,1)} %fusion.31, bf16[256,64,256]{0,2,1:T(8,128)(2,1)} %copy.43, bf16[256,256]{1,0:T(8,128)(2,1)S(1)} %copy-done.2), kind=kOutput, calls=%fused_computation.38 | convolution fusion | flops 2168455168 | bytes 25296896 | tf_op jit(solution)/shard_map/pi,sijc->spjc/dot_general | solution.py:25
  341.9 12.2 %copy.44 = bf16[1,256,64,256]{3,2,0,1:T(8,128)(2,1)} copy(bf16[1,256,64,256]{1,3,2,0:T(8,128)(2,1)} %convert_bitcast_fusion.3) | data formatting | bytes 16777216 | tf_op jit(solution)/shard_map/convert_element_type | solution.py:27
  354.2 5.7 all-to-all-start.1
  359.9 14.2 %convert_bitcast_fusion.1 = bf16[1,256,64,256]{1,3,2,0:T(8,128)(2,1)} fusion(f32[64,256,256]{2,1,0:T(8,128)} %copy-done.1, bf16[256,64,256]{0,2,1:T(8,128)(2,1)} %copy.43, bf16[256,256]{1,0:T(8,128)(2,1)S(1)} %copy-done.3), kind=kOutput, calls=%fused_computation.36 | convolution fusion | flops 2164260864 | bytes 33685504 | tf_op jit(solution)/shard_map/ia,sijc->sajc/dot_general | solution.py:48
  374.1 12.2 %copy.52 = bf16[1,256,64,256]{3,2,0,1:T(8,128)(2,1)} copy(bf16[1,256,64,256]{1,3,2,0:T(8,128)(2,1)} %convert_bitcast_fusion.1) | data formatting | bytes 16777216 | tf_op jit(solution)/shard_map/convert_element_type | solution.py:50
  386.3 66.7 %all-to-all-done.1 = bf16[1,256,64,256]{3,2,0,1:T(8,128)(2,1)} async-done(((bf16[1,256,64,256]{3,2,0,1:T(8,128)(2,1)}), bf16[1,256,64,256]{3,2,0,1:T(8,128)(2,1)}, u32[]{:S(2)}, u32[]{:S(2)}) %all-to-all-start.1) | async-done | bytes 8388640 | tf_op jit(solution)/shard_map/all_to_all | solution.py:28
  453.0 5.9 all-to-all-start.3
  459.0 8.5 %copy.45 = bf16[1,64,4,64,256]{4,3,2,1,0:T(8,128)(2,1)} copy(bf16[1,64,4,64,256]{4,3,1,2,0:T(8,128)(2,1)} %bitcast.16) | data formatting | bytes 16777216 | tf_op jit(solution)/shard_map/all_to_all | solution.py:28
  467.5 84.6 %all-to-all-done.3 = bf16[1,256,64,256]{3,2,0,1:T(8,128)(2,1)} async-done(((bf16[1,256,64,256]{3,2,0,1:T(8,128)(2,1)}), bf16[1,256,64,256]{3,2,0,1:T(8,128)(2,1)}, u32[]{:S(2)}, u32[]{:S(2)}) %all-to-all-start.3) | async-done | bytes 8388640 | tf_op jit(solution)/shard_map/all_to_all | solution.py:51
  552.1 8.4 %copy.53 = bf16[1,64,4,64,256]{4,3,2,1,0:T(8,128)(2,1)} copy(bf16[1,64,4,64,256]{4,3,1,2,0:T(8,128)(2,1)} %bitcast.36) | data formatting | bytes 16777216 | tf_op jit(solution)/shard_map/all_to_all | solution.py:51
  560.5 23.0 %fusion.11 = (f32[1,64,256,256]{3,2,1,0:T(8,128)}, bf16[1,64,256,256]{3,2,1,0:T(8,128)(2,1)}) fusion(f32[1,64,256,256]{3,2,1,0:T(8,128)} %bitcast.145, f32[256]{0:T(256)S(1)} %copy-done.5, bf16[1,16384,256]{2,1,0:T(8,128)(2,1)} %param.8, bf16[64,256,256]{2,1,0:T(8,128)(2,1)} %bitcast.151, bf16[256,256]{1,0:T(8,128)(2,1)S(1)} %copy-done), kind=kOutput, calls=%fused_computation.15 | convolution fusion | flops 2206203904 | bytes 58852352 | tf_op jit(solution)/shard_map/qj,spjc->spqc/dot_general | solution.py:29
  583.4 0.0 copy-start.4
  583.4 10.1 %fusion.12 = f32[256]{0:T(256)S(1)} fusion(f32[1,64,256,256]{3,2,1,0:T(8,128)} %get-tuple-element.12, bf16[1,64,256,256]{3,2,1,0:T(8,128)(2,1)} %bitcast.142), kind=kLoop, calls=%fused_computation.16 | loop fusion | flops 12582656 | bytes 25166848 | tf_op jit(solution)/shard_map/reduce_sum | solution.py:57
  593.5 40.2 %psum.7 = f32[256]{0:T(256)S(1)} all-reduce(f32[256]{0:T(256)S(1)} %fusion.12), channel_id=1, replica_groups=mesh['scene'=8,'seq'=4] {'scene','seq'}, use_global_device_ids=true, to_apply=%region_2.0 | all-reduce | flops 256 | bytes 2048 | tf_op jit(solution)/shard_map/psum | solution.py:58
  633.7 0.6 broadcast_multiply_fusion
  634.3 0.0 copy-done.4
  634.3 12.3 %fusion.13 = bf16[1,64,256,256]{3,2,1,0:T(8,128)(2,1)} fusion(f32[1,64,256,256]{3,2,1,0:T(8,128)} %get-tuple-element.12, bf16[64,256,256]{2,1,0:T(8,128)(2,1)} %bitcast.146, f32[256]{0:T(256)S(1)} %copy-done.5, bf16[256,256]{1,0:T(8,128)(2,1)S(1)} %copy-done.4), kind=kOutput, calls=%fused_computation.18 | convolution fusion | flops 2160066560 | bytes 33686528 | tf_op jit(solution)/shard_map/jb,sajc->sabc/dot_general | solution.py:53
  646.6 0.0 reduce-scatter.2.cloned.1.call-done
Async XLA Ops:
  7.2 65.9 %copy-start = (bf16[256,256]{1,0:T(8,128)(2,1)S(1)}, bf16[256,256]{1,0:T(8,128)(2,1)}, u32[]{:S(2)}) copy-start(bf16[256,256]{1,0:T(8,128)(2,1)} %param.15) | copy-start | bytes 393220
  28.5 99.4 %all-to-all-start = ((bf16[1,64,256,256]{3,1,0,2:T(8,128)(2,1)}), bf16[1,64,256,256]{3,1,0,2:T(8,128)(2,1)}, u32[]{:S(2)}, u32[]{:S(2)}) async-start(bf16[1,64,256,256]{3,1,0,2:T(8,128)(2,1)} %copy.39), calls=%async_computation | async-start | bytes 16777216 | tf_op jit(solution)/shard_map/all_to_all | solution.py:20
  55.7 17.5 %copy-start.5 = (f32[256]{0:T(256)S(1)}, f32[256]{0:T(256)}, u32[]{:S(2)}) copy-start(f32[256]{0:T(256)} %param.10) | copy-start | bytes 3076
  127.9 98.8 %all-to-all-start.2 = ((bf16[1,64,256,256]{3,1,0,2:T(8,128)(2,1)}), bf16[1,64,256,256]{3,1,0,2:T(8,128)(2,1)}, u32[]{:S(2)}, u32[]{:S(2)}) async-start(bf16[1,64,256,256]{3,1,0,2:T(8,128)(2,1)} %copy.48), calls=%async_computation.2 | async-start | bytes 16777216 | tf_op jit(solution)/shard_map/all_to_all | solution.py:41
  133.6 513.0 %reduce-scatter.2.cloned.1.call-start = ((), (), s32[]{:S(2)}) async-start(), calls=%async_computation.5 | async-start | bytes 18874368 | tf_op jit(solution)/shard_map/reduce_scatter | solution.py:46
  238.3 8.3 %copy-start.3 = (bf16[256,256]{1,0:T(8,128)(2,1)S(1)}, bf16[256,256]{1,0:T(8,128)(2,1)}, u32[]{:S(2)}) copy-start(bf16[256,256]{1,0:T(8,128)(2,1)} %param.13) | copy-start | bytes 393220
  246.6 23.9 %copy-start.2 = (bf16[256,256]{1,0:T(8,128)(2,1)S(1)}, bf16[256,256]{1,0:T(8,128)(2,1)}, u32[]{:S(2)}) copy-start(bf16[256,256]{1,0:T(8,128)(2,1)} %param.14) | copy-start | bytes 393220
  284.1 5.7 copy-start.1
  354.2 98.9 %all-to-all-start.1 = ((bf16[1,256,64,256]{3,2,0,1:T(8,128)(2,1)}), bf16[1,256,64,256]{3,2,0,1:T(8,128)(2,1)}, u32[]{:S(2)}, u32[]{:S(2)}) async-start(bf16[1,256,64,256]{3,2,0,1:T(8,128)(2,1)} %copy.44), calls=%async_computation.1 | async-start | bytes 16777216 | tf_op jit(solution)/shard_map/all_to_all | solution.py:28
  453.0 99.1 %all-to-all-start.3 = ((bf16[1,256,64,256]{3,2,0,1:T(8,128)(2,1)}), bf16[1,256,64,256]{3,2,0,1:T(8,128)(2,1)}, u32[]{:S(2)}, u32[]{:S(2)}) async-start(bf16[1,256,64,256]{3,2,0,1:T(8,128)(2,1)} %copy.52), calls=%async_computation.3 | async-start | bytes 16777216 | tf_op jit(solution)/shard_map/all_to_all | solution.py:51
  583.4 50.9 %copy-start.4 = (bf16[256,256]{1,0:T(8,128)(2,1)S(1)}, bf16[256,256]{1,0:T(8,128)(2,1)}, u32[]{:S(2)}) copy-start(bf16[256,256]{1,0:T(8,128)(2,1)} %param.12) | copy-start | bytes 393220
Sparse Core Ops, SparseCore 0:
  317.7 283.8 reduce-scatter.1
where the time goes:
time: 662 us; the launch traced here: 654 us
  waiting for transfers between devices  254 us (38%)
  local copies, waits for them, and re-layouts  171 us (26%)
  matrix products  120 us (18%)
  blocking collectives  40.2 us (6%)
  other arithmetic  30.2 us (5%)
  starting transfers between devices  23.2 us (4%)
  between operations  14.5 us (2%)
    all_to_all x1, waiting for transfers between devices, on_device(): lax.all_to_all(grad_first, 'seq', split_axis=1, concat_axis=2, tiled=True)  84.6 us
    all_to_all x1, waiting for transfers between devices, on_device(): lax.all_to_all(grad_unmixed, 'seq', split_axis=2, concat_axis=1, tiled=True)  72.9 us
    all_to_all x1, waiting for transfers between devices, on_device(): lax.all_to_all(unmixed, 'seq', split_axis=1, concat_axis=2, tiled=True)  66.7 us
    psum x1, blocking collectives, on_device(): gain_total = lax.psum(gain_term, ('scene', 'seq'))  40.2 us
    all_to_all x1, waiting for transfers between devices, on_device(): lax.all_to_all(first_mix, 'seq', split_axis=2, concat_axis=1, tiled=True)  29.7 us
    dot_general x1, matrix products, on_device(): jnp.einsum('ia,sajc->sijc', across_mix, spread_mix, preferred_element_typ...  23.9 us
    dot_general x1, matrix products, on_device(): jnp.einsum('qj,spjc->spqc', block_unmix, returned, preferred_element_type...  23 us
    all_to_all x2, local copies, waits for them, and re-layouts, on_device(): lax.all_to_all(first_mix, 'seq', split_axis=2, concat_axis=1, tiled=True)  20 us
  transfers between devices with their start and end apart: 5, of which 4 were waited for; matrix products, arithmetic and copies ran while one was open for 32% of the time, Pallas kernels for 0%

commit v1 on v0

v1 whole, which is shorter than its diff:
```python
import functools

import jax
import jax.numpy as jnp
from jax import lax
from jax.experimental import pallas as pl
from jax.experimental.pallas import tpu as pltpu
from jax.sharding import PartitionSpec as P

f32 = jnp.float32
bf16 = jnp.bfloat16
T = 16


def dot(a, b):
    return jnp.dot(a, b, preferred_element_type=f32)


def turn(swap_ref, block):
    c = block.shape[-1]
    return dot(swap_ref[...], block.reshape(T * T, c)).astype(bf16).reshape(T, T, c)


def at(i):
    return pl.ds(pl.multiple_of(i * T, T), T)


def loop(count, body, unroll=4):
    def step(i, carry):
        body(i)
        return carry

    lax.fori_loop(0, count, step, 0, unroll=min(unroll, count))


def turn_out(swap_ref, held_ref, out_refs):
    groups = out_refs[0].shape[0] // T
    for o, out_ref in enumerate(out_refs):

        def body(g, o=o, out_ref=out_ref):
            out_ref[at(g)] = turn(swap_ref, held_ref[:, at(o * groups + g), :])

        loop(groups, body)


def mix_kernel(x_ref, w_ref, swap_ref, *rest):
    out_refs, held_ref = rest[:-1], rest[-1]

    def body(a):
        held_ref[a] = dot(w_ref[...], x_ref[a]).astype(bf16)

    loop(T, body)
    turn_out(swap_ref, held_ref, out_refs)


def grad_mix_kernel(x_ref, e_ref, gain_ref, w_ref, swap_ref, *rest):
    out_refs, held_ref = rest[:-1], rest[-1]
    gain = gain_ref[...]

    def body(a):
        g = x_ref[a].astype(f32) * gain
        dv = (e_ref[a].astype(f32) * g * jax.nn.sigmoid(g)).astype(bf16)
        held_ref[a] = dot(w_ref[...], dv).astype(bf16)

    loop(T, body, 2)
    turn_out(swap_ref, held_ref, out_refs)


def across_kernel(n, *refs):
    in_refs, (k_ref, f_ref, g_ref, swap_ref) = refs[:n], refs[n : n + 4]
    out_refs, (y_ref, kt_ref, held_ref) = refs[n + 4 : 2 * n + 4], refs[2 * n + 4 :]

    def turn_kernel(i):
        kt_ref[:, at(i), :] = turn(swap_ref, k_ref[at(i)])

    loop(k_ref.shape[0] // T, turn_kernel)

    def body(j):
        y1 = jnp.concatenate([r[j] for r in in_refs], axis=0)
        y2 = dot(f_ref[...], y1).astype(bf16)
        y_ref[j] = y2
        z = (y2.astype(f32) * kt_ref[j].astype(f32)).astype(bf16)
        held_ref[j] = dot(g_ref[...], z).astype(bf16)

    loop(T, body)
    turn_out(swap_ref, held_ref, out_refs)


def grad_across_kernel(n, *refs):
    in_refs, (y_ref, kt_ref, f_ref, g_ref, swap_ref) = refs[:n], refs[n : n + 5]
    out_refs, (term_ref, held_ref, held_term_ref) = refs[n + 5 : 2 * n + 5], refs[2 * n + 5 :]

    def body(j):
        dw1 = jnp.concatenate([r[j] for r in in_refs], axis=0)
        dz = dot(g_ref[...], dw1)
        held_term_ref[j] = (dz * y_ref[j].astype(f32)).astype(bf16)
        dy2 = (dz * kt_ref[j].astype(f32)).astype(bf16)
        held_ref[j] = dot(f_ref[...], dy2).astype(bf16)

    loop(T, body)
    turn_out(swap_ref, held_term_ref, (term_ref,))
    turn_out(swap_ref, held_ref, out_refs)


def gate_kernel(n, *refs):
    in_refs, (x_ref, e_ref, gain_ref, w_ref) = refs[:n], refs[n : n + 4]
    mixed_ref, dg_ref, sum_ref = refs[n + 4 :]
    gain = gain_ref[...]

    @pl.when(pl.program_id(0) == 0)
    def _():
        sum_ref[...] = jnp.zeros_like(sum_ref)

    def body(p):
        v = dot(w_ref[...], jnp.concatenate([r[p] for r in in_refs], axis=0))
        x = x_ref[p].astype(f32)
        g = x * gain
        s = jax.nn.sigmoid(g)
        vs = v * s
        mixed_ref[p] = (vs * g).astype(bf16)
        dg = e_ref[p].astype(f32) * vs * (1.0 + g * (1.0 - s))
        sum_ref[...] += jnp.sum((x * dg).reshape(-1, 8, x.shape[-1]), axis=0)
        dg_ref[p] = (dg * gain).astype(bf16)

    loop(x_ref.shape[0], body, 2)


def grad_in_kernel(n, *refs):
    in_refs, (dg_ref, w_ref, out_ref) = refs[:n], refs[n:]

    def body(a):
        dy1 = jnp.concatenate([r[a] for r in in_refs], axis=0)
        out_ref[a] = (dot(w_ref[...], dy1) + dg_ref[a].astype(f32)).astype(bf16)

    loop(out_ref.shape[0], body)


def lead(rows, shape):
    return pl.BlockSpec((rows,) + tuple(shape[1:]), lambda i: (i,) + (0,) * (len(shape) - 1))


def second(shape):
    return pl.BlockSpec((shape[0], T, shape[2]), lambda i: (0, i, 0))


def whole(shape):
    return pl.BlockSpec(tuple(shape), lambda i: (0,) * len(shape))


def run(body, grid, args, in_specs, outs, out_specs, scratch, products, name):
    shapes = [jax.ShapeDtypeStruct(s, t) for s, t in outs]
    moved = sum(x.size * x.dtype.itemsize for x in args) + sum(
        x.size * x.dtype.itemsize for x in shapes
    )
    return pl.pallas_call(
        body,
        grid=(grid,),
        in_specs=in_specs,
        out_specs=out_specs,
        out_shape=shapes,
        scratch_shapes=scratch,
        name=name,
        compiler_params=pltpu.CompilerParams(
            vmem_limit_bytes=48 * 1024 * 1024, dimension_semantics=("arbitrary",)
        ),
        cost_estimate=pl.CostEstimate(
            flops=int(products), bytes_accessed=int(moved), transcendentals=0
        ),
    )(*args)


def on_device(
    scene_x, cotangent, gate_gain, kernel, block_mix, across_mix, across_unmix, block_unmix
):
    n = lax.axis_size("seq")
    me = lax.axis_index("seq")
    _, row_count, c = scene_x.shape
    size = block_mix.shape[0]
    across = across_mix.shape[0]
    la = row_count // size
    lj = size // n
    x = scene_x.reshape(la, size, c)
    e = cotangent.reshape(la, size, c)
    gain = gate_gain.reshape(1, c)

    rows = jnp.arange(size)
    pick_j = ((((rows // lj) ^ me) * lj + rows % lj)[:, None] == rows[None, :]).astype(bf16)
    rows = jnp.arange(across)
    pick_a = ((((rows // la) ^ me) * la + rows % la)[:, None] == rows[None, :]).astype(bf16)
    f1 = dot(pick_j, block_mix).astype(bf16)
    g1_t = dot(pick_j, block_unmix.T).astype(bf16)
    g2 = dot(pick_a, across_unmix).astype(bf16)
    f2_t = dot(pick_a, across_mix.T).astype(bf16)
    rows = jnp.arange(T * T)
    swap = ((rows % T * T + rows // T)[:, None] == rows[None, :]).astype(bf16)

    def exchange(parts):
        return [parts[0]] + [
            lax.ppermute(parts[o], "seq", [(i, i ^ o) for i in range(n)]) for o in range(1, n)
        ]

    products = 2 * la * size * size * c
    sq = whole((size, size))
    sw = whole((T * T, T * T))
    one = whole((1, c))
    held_j = pltpu.VMEM((T, size, c), bf16)
    held_a = pltpu.VMEM((T, across, c), bf16)
    by_j = (lj, la, c)
    by_a = (la, lj, c)

    y1 = run(
        mix_kernel, la // T, (x, f1, swap), [lead(T, x.shape), sq, sw],
        [(by_j, bf16)] * n, [second(by_j)] * n, [held_j], 2 * products, "mix",
    )
    y1_in = exchange(y1)
    dw1 = run(
        grad_mix_kernel, la // T, (x, e, gain, g1_t, swap),
        [lead(T, x.shape), lead(T, x.shape), one, sq, sw],
        [(by_j, bf16)] * n, [second(by_j)] * n, [held_j], 2 * products, "grad_mix",
    )
    dw1_in = exchange(dw1)

    ij = (across, lj, c)
    ji = (lj, across, c)
    aq = whole((across, across))
    got = run(
        functools.partial(across_kernel, n), lj // T, (*y1_in, kernel, f2_t.T, g2, swap),
        [lead(T, by_j)] * n + [second(ij), aq, aq, sw],
        [(by_a, bf16)] * n + [(ji, bf16)] * 2, [second(by_a)] * n + [lead(T, ji)] * 2,
        [held_a], 4 * products, "across",
    )
    w1, (y2, kernel_t) = got[:n], got[n:]
    w1_in = exchange(w1)
    got = run(
        functools.partial(grad_across_kernel, n), lj // T,
        (*dw1_in, y2, kernel_t, f2_t, g2.T, swap),
        [lead(T, by_j)] * n + [lead(T, ji)] * 2 + [aq, aq, sw],
        [(by_a, bf16)] * n + [(ij, bf16)], [second(by_a)] * n + [second(ij)],
        [held_a, held_a], 4 * products, "grad_across",
    )
    dy1, term = got[:n], got[n]
    kernel_grad = lax.psum_scatter(term, "scene", scatter_dimension=0, tiled=True)
    dy1_in = exchange(dy1)

    step = min(8, la)
    mixed, dg, sums = run(
        functools.partial(gate_kernel, n), la // step, (*w1_in, x, e, gain, g1_t.T),
        [lead(step, by_a)] * n + [lead(step, x.shape)] * 2 + [one, sq],
        [(x.shape, bf16), (x.shape, bf16), ((8, c), f32)],
        [lead(step, x.shape)] * 2 + [whole((8, c))], [], 4 * products, "gate",
    )
    gain_total = lax.psum(jnp.sum(sums, axis=0), ("scene", "seq"))
    total_rows = lax.axis_size("scene") * la * n * size
    grad_scale = 1.0 / jnp.sqrt(jnp.float32(total_rows))
    (grad_x,) = run(
        functools.partial(grad_in_kernel, n), la // step, (*dy1_in, dg, f1.T),
        [lead(step, by_a)] * n + [lead(step, x.shape), sq],
        [(x.shape, bf16)], [lead(step, x.shape)], [], products, "grad_in",
    )
    return (
        mixed.reshape(scene_x.shape),
        grad_x.reshape(scene_x.shape),
        kernel_grad.astype(f32),
        gain_total * grad_scale,
    )


def solution(mesh):
    return jax.shard_map(
        on_device,
        mesh=mesh,
        in_specs=(
            P("scene", "seq", None),
            P("scene", "seq", None),
            P(),
            P(None, "seq", None),
            P(),
            P(),
            P(),
            P(),
        ),
        out_specs=(P("scene", "seq", None), P("scene", "seq", None), P("scene", "seq", None), P()),
        check_vma=False,
    )
```

time: 662 us -> 469 us (0.71); the launches traced: 654 us -> 469 us
  local copies, waits for them, and re-layouts: 171 us -> 12.1 us
  matrix products: 120 us -> 1.04 us
  Pallas kernels: 0 us -> 105 us
  blocking collectives: 40.2 us -> 102 us
  waiting for transfers between devices: 254 us -> 221 us
  other arithmetic: 30.2 us -> 3.5 us
  starting transfers between devices: 23.2 us -> 10.4 us
    all_to_all x4 -> x0, waiting for transfers between devices: 254 us -> none  [the longest x1 84.6 us: on_device(): lax.all_to_all(grad_first, 'seq', split_axis=1, concat_axis=2, tiled=True)]
    ppermute x0 -> x12, waiting for transfers between devices: none -> 221 us  [exchange(): lax.ppermute(parts[o], 'seq', [(i, i ^ o) for i in range(n)])]
    dot_general x8 -> x4, matrix products: 120 us -> 1.04 us  [dot(): return jnp.dot(a, b, preferred_element_type=f32)]
    pallas_call x0 -> x6, Pallas kernels: none -> 105 us  [run(): pl.pallas_call(body, grid=(grid,), in_specs=in_specs, out_specs=out_specs...]
    convert_element_type x5 -> x4, local copies, waits for them, and re-layouts: 66.3 us -> 0.39 us  [the longest x1 0.1 us: on_device(): f1 = dot(pick_j, block_mix).astype(bf16)]
    psum x1, blocking collectives: 40.2 us -> 102 us  [on_device(): gain_total = lax.psum(jnp.sum(sums, axis=0), ('scene', 'seq'))]
    all_to_all x6 -> x0, local copies, waits for them, and re-layouts: 56.7 us -> none  [the longest x2 20 us: on_device(): lax.all_to_all(first_mix, 'seq', split_axis=2, concat_axis=1, tiled=True)]
    all_to_all x4 -> x0, starting transfers between devices: 22.9 us -> none  [the longest x1 5.91 us: on_device(): lax.all_to_all(grad_first, 'seq', split_axis=1, concat_axis=2, tiled=True)]
  transfers between devices with their start and end apart: 5 -> 13, of which waited for: 4 -> 7; matrix products, arithmetic and copies ran while one was open for 32% -> 0% of each run, Pallas kernels for 0% -> 15%
where the time goes in v1:
time: 469 us
  waiting for transfers between devices  221 us (47%)
  Pallas kernels  105 us (22%)
  blocking collectives  102 us (22%)
  between operations  14.2 us (3%)
  local copies, waits for them, and re-layouts  12.1 us (3%)
  starting transfers between devices  10.4 us (2%)
    ppermute x12, waiting for transfers between devices, exchange(): lax.ppermute(parts[o], 'seq', [(i, i ^ o) for i in range(n)])  221 us
    pallas_call x6, Pallas kernels, run(): pl.pallas_call(body, grid=(grid,), in_specs=in_specs, out_specs=out_specs...  105 us
    psum x1, blocking collectives, on_device(): gain_total = lax.psum(jnp.sum(sums, axis=0), ('scene', 'seq'))  102 us
    unnamed x30, local copies, waits for them, and re-layouts  11.7 us
    ppermute x12, starting transfers between devices, exchange(): lax.ppermute(parts[o], 'seq', [(i, i ^ o) for i in range(n)])  10.4 us
  transfers between devices with their start and end apart: 13, of which 7 were waited for; matrix products, arithmetic and copies ran while one was open for 0% of the time, Pallas kernels for 15%

profile of v1, /device:TPU:0, one launch (start us, length us, event | category | flops | bytes accessed | tf_op | source)
XLA Modules:
  0.0 468.8 jit_solution(13602046971992850010)
XLA Ops:
  7.2 0.0 copy-start
  7.2 0.0 reduce-scatter.2.cloned.1.call-start
  7.3 0.1 fusion.swap_ref.refs_7_.refs_8_
  7.4 0.7 copy-done
  8.1 0.3 convolution_convert_fusion.3
  8.4 0.1 copy.13.w_ref
  8.5 0.0 copy-start.11
  8.5 0.0 copy-start.2
  8.5 10.7 %mix.1 = (bf16[64,64,256]{2,1,0:T(8,128)(2,1)S(1)}, bf16[64,64,256]{2,1,0:T(8,128)(2,1)S(1)}, bf16[64,64,256]{2,1,0:T(8,128)(2,1)}, bf16[64,64,256]{2,1,0:T(8,128)(2,1)}) custom-call(bf16[64,256,256]{2,1,0:T(8,128)(2,1)} %bitcast.20, bf16[256,256]{1,0:T(8,128)(2,1)S(1)} %copy.13.w_ref, bf16[256,256]{1,0:T(8,128)(2,1)S(1)} %fusion.swap_ref.refs_7_.refs_8_), custom_call_target="tpu_custom_call" | custom-call | flops 4294967296 | bytes 17039360 | tf_op jit(solution)/shard_map/mix/pallas_call | solution.py:155
  19.2 1.3 copy-done.10
  20.5 0.5 collective-permute-start
  21.0 2.5 collective-permute-start.1
  23.5 0.1 collective-permute-start.2
  23.6 0.0 copy-done.11
  23.6 0.2 convolution_convert_fusion.w_ref
  23.8 0.0 copy-done.2
  23.9 0.0 copy-start.12
  23.9 0.0 copy-start.13
  23.9 17.1 %grad_mix.1 = (bf16[64,64,256]{2,1,0:T(8,128)(2,1)S(1)}, bf16[64,64,256]{2,1,0:T(8,128)(2,1)}, bf16[64,64,256]{2,1,0:T(8,128)(2,1)}, bf16[64,64,256]{2,1,0:T(8,128)(2,1)}) custom-call(bf16[64,256,256]{2,1,0:T(8,128)(2,1)} %bitcast.21, bf16[64,256,256]{2,1,0:T(8,128)(2,1)} %bitcast.23, f32[1,256]{1,0:T(1,128)S(1)} %bitcast.17, ...), custom_call_target="tpu_custom_call" | custom-call | flops 4294967296 | bytes 25428992 | tf_op jit(solution)/shard_map/grad_mix/pallas_call | solution.py:155
  41.0 1.3 copy-done.5
  42.3 0.1 collective-permute-start.6
  42.4 1.9 collective-permute-start.7
  44.3 0.0 collective-permute-done.refs_1_
  44.3 0.0 collective-permute-start.8
  44.3 0.0 copy-done.12
  44.3 0.2 convolution_convert_fusion.2.refs_6_
  44.6 1.1 copy-done.14
  45.7 0.1 copy.15.refs_5_
  45.8 0.3 convolution_convert_fusion.1
  46.1 0.1 copy.16.refs_6_
  46.2 24.1 %collective-permute-done.1.refs_2_ = bf16[64,64,256]{2,1,0:T(8,128)(2,1)} collective-permute-done((bf16[64,64,256]{2,1,0:T(8,128)(2,1)}, bf16[64,64,256]{2,1,0:T(8,128)(2,1)}, u32[]{:S(2)}, u32[]{:S(2)}) %collective-permute-start.1) | collective-permute-done | bytes 2097184 | tf_op jit(solution)/shard_map/ppermute | solution.py:199
  70.3 44.6 %collective-permute-done.2.refs_3_ = bf16[64,64,256]{2,1,0:T(8,128)(2,1)} collective-permute-done((bf16[64,64,256]{2,1,0:T(8,128)(2,1)}, bf16[64,64,256]{2,1,0:T(8,128)(2,1)}, u32[]{:S(2)}, u32[]{:S(2)}) %collective-permute-start.2) | collective-permute-done | bytes 2097184 | tf_op jit(solution)/shard_map/ppermute | solution.py:199
  114.8 22.8 %across.1 = (bf16[64,64,256]{2,1,0:T(8,128)(2,1)S(1)}, bf16[64,64,256]{2,1,0:T(8,128)(2,1)S(1)}, bf16[64,64,256]{2,1,0:T(8,128)(2,1)}, bf16[64,64,256]{2,1,0:T(8...) custom-call(bf16[64,64,256]{2,1,0:T(8,128)(2,1)} %copy-done.10, ...), custom_call_target="tpu_custom_call" | custom-call | flops 8589934592 | bytes 42336256 | tf_op jit(solution)/shard_map/across/pallas_call | solution.py:155
  137.6 1.3 copy-done.8
  139.0 0.0 collective-permute-done.6.refs_1_
  139.0 21.2 %collective-permute-done.7.refs_2_ = bf16[64,64,256]{2,1,0:T(8,128)(2,1)} collective-permute-done((bf16[64,64,256]{2,1,0:T(8,128)(2,1)}, bf16[64,64,256]{2,1,0:T(8,128)(2,1)}, u32[]{:S(2)}, u32[]{:S(2)}) %collective-permute-start.7) | collective-permute-done | bytes 2097184 | tf_op jit(solution)/shard_map/ppermute | solution.py:199
  160.1 44.6 %collective-permute-done.8.refs_3_ = bf16[64,64,256]{2,1,0:T(8,128)(2,1)} collective-permute-done((bf16[64,64,256]{2,1,0:T(8,128)(2,1)}, bf16[64,64,256]{2,1,0:T(8,128)(2,1)}, u32[]{:S(2)}, u32[]{:S(2)}) %collective-permute-start.8) | collective-permute-done | bytes 2097184 | tf_op jit(solution)/shard_map/ppermute | solution.py:199
  204.7 22.5 %grad_across.1 = (bf16[64,64,256]{2,1,0:T(8,128)(2,1)S(1)}, bf16[64,64,256]{2,1,0:T(8,128)(2,1)S(1)}, bf16[64,64,256]{2,1,0:T(8,128)(2,1)}, bf16[64,64,256]{2,1,0:T(8,128)(2,1)}, bf16[256,64,256]{2,1,0:T(8,128)(2,1)}) custom-call(bf16[64,64,256]{2,1,0:T(8,128)(2,1)} %copy-done.5, bf16[64,64,256]{2,1,0:T(8,128)(2,1)} %collective-permute-done.6.refs_1_, ...), custom_call_target="tpu_custom_call" | custom-call | flops 8589934592 | bytes 42336256 | tf_op jit(solution)/shard_map/grad_across/pallas_call | solution.py:155
  227.2 0.0 copy-done.4
  227.2 1.4 copy-done.3
  228.5 0.0 reduce-scatter.2.cloned.1.call-update
  228.6 0.2 collective-permute-start.3
  228.8 1.6 collective-permute-start.4
  230.4 0.1 collective-permute-start.5
  230.5 0.4 collective-permute-start.9
  230.9 1.6 collective-permute-start.10
  232.5 0.5 collective-permute-done.3.refs_1_
  233.0 1.3 copy-done.6
  234.3 1.4 collective-permute-start.11
  235.7 0.1 copy.17.refs_7_
  235.8 41.8 %collective-permute-done.4.refs_2_ = bf16[64,64,256]{2,1,0:T(8,128)(2,1)} collective-permute-done((bf16[64,64,256]{2,1,0:T(8,128)(2,1)}, bf16[64,64,256]{2,1,0:T(8,128)(2,1)}, u32[]{:S(2)}, u32[]{:S(2)}) %collective-permute-start.4) | collective-permute-done | bytes 2097184 | tf_op jit(solution)/shard_map/ppermute | solution.py:199
  277.5 44.1 %collective-permute-done.5.refs_3_ = bf16[64,64,256]{2,1,0:T(8,128)(2,1)} collective-permute-done((bf16[64,64,256]{2,1,0:T(8,128)(2,1)}, bf16[64,64,256]{2,1,0:T(8,128)(2,1)}, u32[]{:S(2)}, u32[]{:S(2)}) %collective-permute-start.5) | collective-permute-done | bytes 2097184 | tf_op jit(solution)/shard_map/ppermute | solution.py:199
  321.6 1.6 copy-done.7
  323.2 1.6 copy-done.9
  324.8 19.6 %gate.1 = (bf16[64,256,256]{2,1,0:T(8,128)(2,1)}, bf16[64,256,256]{2,1,0:T(8,128)(2,1)}, f32[8,256]{1,0:T(8,128)S(1)}) custom-call(bf16[64,64,256]{2,1,0:T(8,128)(2,1)S(1)} %copy-done.9, bf16[64,64,256]{2,1,0:T(8,128)(2,1)S(1)} %copy-done.7, bf16[64,64,256]{2,1,0:T(8,128)(2,1)} %collective-permute-done.4.refs_2_, ...), custom_call_target="tpu_custom_call" | custom-call | flops 8589934592 | bytes 42083328 | tf_op jit(solution)/shard_map/gate/pallas_call | solution.py:155
  344.4 101.8 %psum.7 = f32[256]{0:T(256)S(1)} all-reduce(f32[256]{0:T(256)S(1)} %reduce_sum.9), channel_id=1, replica_groups=mesh['scene'=8,'seq'=4] {'scene','seq'}, use_global_device_ids=true, to_apply=%region_2.3 | all-reduce | flops 256 | bytes 2048 | tf_op jit(solution)/shard_map/psum | solution.py:252
  446.2 0.0 collective-permute-done.9.refs_1_
  446.2 0.0 collective-permute-done.10.refs_2_
  446.2 0.0 collective-permute-done.11.refs_3_
  446.2 0.0 copy-start.1
  446.3 12.3 %grad_in.1 = bf16[64,256,256]{2,1,0:T(8,128)(2,1)} custom-call(bf16[64,64,256]{2,1,0:T(8,128)(2,1)S(1)} %get-tuple-element.41.refs_0_, bf16[64,64,256]{2,1,0:T(8,128)(2,1)} %collective-permute-done.9.refs_1_, bf16[64,64,256]{2,1,0:T(8,128)(2,1)} %collective-permute-done.10.refs_2_, bf16[64,64,256]{2,1,0:T(8,128)(2,1)} %collective-permute-done.11.refs_3_, ...), custom_call_target="tpu_custom_call" | custom-call | flops 2147483648 | bytes 25296896 | tf_op jit(solution)/shard_map/grad_in/pallas_call | solution.py:155
  458.5 0.6 broadcast_multiply_fusion
  459.1 2.8 convert_element_type.43
  461.9 0.0 copy-done.1
  (14 shorter events, 0.0 us)
Async XLA Ops:
  7.2 0.9 copy-start
  7.2 451.9 %reduce-scatter.2.cloned.1.call-start = ((), (), s32[]{:S(2)}) async-start(), calls=%async_computation.1 | async-start | bytes 9437184 | tf_op jit(solution)/shard_map/reduce_scatter | solution.py:242
  8.5 15.1 %copy-start.11 = (bf16[256,256]{1,0:T(8,128)(2,1)S(1)}, bf16[256,256]{1,0:T(8,128)(2,1)}, u32[]{:S(2)}) copy-start(bf16[256,256]{1,0:T(8,128)(2,1)} %param.15) | copy-start | bytes 393220
  8.5 15.4 %copy-start.2 = (f32[256]{0:T(256)S(1)}, f32[256]{0:T(256)}, u32[]{:S(2)}) copy-start(f32[256]{0:T(256)} %param.10) | copy-start | bytes 3076
  19.2 1.3 copy-start.10
  20.5 23.8 %collective-permute-start = (bf16[64,64,256]{2,1,0:T(8,128)(2,1)S(1)}, bf16[64,64,256]{2,1,0:T(8,128)(2,1)S(1)}, u32[]{:S(2)}, u32[]{:S(2)}) collective-permute-start(bf16[64,64,256]{2,1,0:T(8,128)(2,1)S(1)} %get-tuple-element.27), channel_id=1, source_target_pairs={{0,1},{1,0},{2,3},{3,2},{4,5},{5,4},{6,7},{7,6},{8,9},{9,8},{10,11... | collective-permute-start | bytes 6291464 | tf_op jit(solution)/shard_map/ppermute | solution.py:199
  21.0 49.3 %collective-permute-start.1 = (bf16[64,64,256]{2,1,0:T(8,128)(2,1)}, bf16[64,64,256]{2,1,0:T(8,128)(2,1)}, u32[]{:S(2)}, u32[]{:S(2)}) collective-permute-start(bf16[64,64,256]{2,1,0:T(8,128)(2,1)} %get-tuple-element.28), channel_id=1, source_target_pairs={{0,2},{1,3},{2,0},{3,1},{4,6},{5,7},{6,4},{7,5},{8,10},{9,11},{10,... | collective-permute-start | bytes 6291464 | tf_op jit(solution)/shard_map/ppermute | solution.py:199
  23.5 91.4 %collective-permute-start.2 = (bf16[64,64,256]{2,1,0:T(8,128)(2,1)}, bf16[64,64,256]{2,1,0:T(8,128)(2,1)}, u32[]{:S(2)}, u32[]{:S(2)}) collective-permute-start(bf16[64,64,256]{2,1,0:T(8,128)(2,1)} %get-tuple-element.29), channel_id=1, source_target_pairs={{0,3},{1,2},{2,1},{3,0},{4,7},{5,6},{6,5},{7,4},{8,11},{9,10},{10,... | collective-permute-start | bytes 6291464 | tf_op jit(solution)/shard_map/ppermute | solution.py:199
  23.9 20.5 %copy-start.12 = (bf16[256,256]{1,0:T(8,128)(2,1)S(1)}, bf16[256,256]{1,0:T(8,128)(2,1)}, u32[]{:S(2)}) copy-start(bf16[256,256]{1,0:T(8,128)(2,1)} %param.13) | copy-start | bytes 393220
  23.9 21.9 %copy-start.13 = (bf16[256,256]{1,0:T(8,128)(2,1)S(1)}, bf16[256,256]{1,0:T(8,128)(2,1)}, u32[]{:S(2)}) copy-start(bf16[256,256]{1,0:T(8,128)(2,1)} %param.14) | copy-start | bytes 393220
  41.0 1.3 copy-start.5
  42.3 96.6 %collective-permute-start.6 = (bf16[64,64,256]{2,1,0:T(8,128)(2,1)}, bf16[64,64,256]{2,1,0:T(8,128)(2,1)}, u32[]{:S(2)}, u32[]{:S(2)}) collective-permute-start(bf16[64,64,256]{2,1,0:T(8,128)(2,1)} %get-tuple-element.36), channel_id=1, source_target_pairs={{0,1},{1,0},{2,3},{3,2},{4,5},{5,4},{6,7},{7,6},{8,9},{9,8},{10,11... | collective-permute-start | bytes 6291464 | tf_op jit(solution)/shard_map/ppermute | solution.py:199
  42.4 117.7 %collective-permute-start.7 = (bf16[64,64,256]{2,1,0:T(8,128)(2,1)}, bf16[64,64,256]{2,1,0:T(8,128)(2,1)}, u32[]{:S(2)}, u32[]{:S(2)}) collective-permute-start(bf16[64,64,256]{2,1,0:T(8,128)(2,1)} %get-tuple-element.37), channel_id=1, source_target_pairs={{0,2},{1,3},{2,0},{3,1},{4,6},{5,7},{6,4},{7,5},{8,10},{9,11},{10,... | collective-permute-start | bytes 6291464 | tf_op jit(solution)/shard_map/ppermute | solution.py:199
  44.3 1.4 copy-start.14
  44.3 160.4 %collective-permute-start.8 = (bf16[64,64,256]{2,1,0:T(8,128)(2,1)}, bf16[64,64,256]{2,1,0:T(8,128)(2,1)}, u32[]{:S(2)}, u32[]{:S(2)}) collective-permute-start(bf16[64,64,256]{2,1,0:T(8,128)(2,1)} %get-tuple-element.38), channel_id=1, source_target_pairs={{0,3},{1,2},{2,1},{3,0},{4,7},{5,6},{6,5},{7,4},{8,11},{9,10},{10,... | collective-permute-start | bytes 6291464 | tf_op jit(solution)/shard_map/ppermute | solution.py:199
  137.6 1.3 copy-start.8
  138.9 88.2 %copy-start.4 = (bf16[64,64,256]{2,1,0:T(8,128)(2,1)}, bf16[64,64,256]{2,1,0:T(8,128)(2,1)S(1)}, u32[]{:S(2)}) copy-start(bf16[64,64,256]{2,1,0:T(8,128)(2,1)S(1)} %get-tuple-element.31) | copy-start | bytes 6291460
  227.2 1.4 copy-start.3
  228.6 4.4 collective-permute-start.3
  228.8 48.8 %collective-permute-start.4 = (bf16[64,64,256]{2,1,0:T(8,128)(2,1)}, bf16[64,64,256]{2,1,0:T(8,128)(2,1)}, u32[]{:S(2)}, u32[]{:S(2)}) collective-permute-start(bf16[64,64,256]{2,1,0:T(8,128)(2,1)} %get-tuple-element.32), channel_id=1, source_target_pairs={{0,2},{1,3},{2,0},{3,1},{4,6},{5,7},{6,4},{7,5},{8,10},{9,11},{10,... | collective-permute-start | bytes 6291464 | tf_op jit(solution)/shard_map/ppermute | solution.py:199
  230.4 91.2 %collective-permute-start.5 = (bf16[64,64,256]{2,1,0:T(8,128)(2,1)}, bf16[64,64,256]{2,1,0:T(8,128)(2,1)}, u32[]{:S(2)}, u32[]{:S(2)}) collective-permute-start(bf16[64,64,256]{2,1,0:T(8,128)(2,1)} %get-tuple-element.33), channel_id=1, source_target_pairs={{0,3},{1,2},{2,1},{3,0},{4,7},{5,6},{6,5},{7,4},{8,11},{9,10},{10,... | collective-permute-start | bytes 6291464 | tf_op jit(solution)/shard_map/ppermute | solution.py:199
  230.5 215.7 %collective-permute-start.9 = (bf16[64,64,256]{2,1,0:T(8,128)(2,1)}, bf16[64,64,256]{2,1,0:T(8,128)(2,1)}, u32[]{:S(2)}, u32[]{:S(2)}) collective-permute-start(bf16[64,64,256]{2,1,0:T(8,128)(2,1)} %copy-done.3), channel_id=1, source_target_pairs={{0,1},{1,0},{2,3},{3,2},{4,5},{5,4},{6,7},{7,6},{8,9},{9,8},{10,11... | collective-permute-start | bytes 6291464 | tf_op jit(solution)/shard_map/ppermute | solution.py:199
  230.9 215.3 %collective-permute-start.10 = (bf16[64,64,256]{2,1,0:T(8,128)(2,1)}, bf16[64,64,256]{2,1,0:T(8,128)(2,1)}, u32[]{:S(2)}, u32[]{:S(2)}) collective-permute-start(bf16[64,64,256]{2,1,0:T(8,128)(2,1)} %get-tuple-element.43), channel_id=1, source_target_pairs={{0,2},{1,3},{2,0},{3,1},{4,6},{5,7},{6,4},{7,5},{8,10},{9,11},{10,... | collective-permute-start | bytes 6291464 | tf_op jit(solution)/shard_map/ppermute | solution.py:199
  233.0 1.3 copy-start.6
  234.3 211.9 %collective-permute-start.11 = (bf16[64,64,256]{2,1,0:T(8,128)(2,1)}, bf16[64,64,256]{2,1,0:T(8,128)(2,1)}, u32[]{:S(2)}, u32[]{:S(2)}) collective-permute-start(bf16[64,64,256]{2,1,0:T(8,128)(2,1)} %get-tuple-element.44), channel_id=1, source_target_pairs={{0,3},{1,2},{2,1},{3,0},{4,7},{5,6},{6,5},{7,4},{8,11},{9,10},{10,... | collective-permute-start | bytes 6291464 | tf_op jit(solution)/shard_map/ppermute | solution.py:199
  321.6 1.6 copy-start.7
  323.2 1.6 copy-start.9
  446.2 15.7 %copy-start.1 = (bf16[256,256]{1,0:T(8,128)(2,1)S(1)}, bf16[256,256]{1,0:T(8,128)(2,1)}, u32[]{:S(2)}) copy-start(bf16[256,256]{1,0:T(8,128)(2,1)} %param.12) | copy-start | bytes 393220
Sparse Core Ops, SparseCore 0:
  228.7 150.2 reduce-scatter.1
